TPU v7x, 32 devices: a whole 2x2x4 slice. The times are simulated.
32 devices in a mesh: groups: 2 (over y), dp: 4 (over z), opt: 4 (over x, core).
Axes of the slice: x: 2, y: 2, z: 4, core: 2. Of those that a mesh axis runs over, the one named last changes fastest.
Arguments:
- gate_pre: bfloat16 [2048, 14336], P(('groups', 'dp'), 'opt'), parts along dimension 0, may hold values from -6 to 6
- up_pre: bfloat16 [2048, 14336], P(('groups', 'dp'), 'opt'), parts along dimension 0, may hold values from -6 to 6
- cotangent: bfloat16 [2048, 4096], P(('groups', 'dp'), 'opt'), parts along dimension 0, may hold values from -6 to 6
- down_weight: bfloat16 [4096, 14336], P('dp', 'opt'), may hold values from -0.046875 to 0.046875
- projector: bfloat16 [8192, 1024], P(('groups', 'opt')), parts along dimension 0, may hold values from -0.09375 to 0.09375
- moment_first: float32 [2048, 14336], P(('groups', 'dp'), 'opt'), parts along dimension 0, may hold values from -6 to 6
- moment_second: float32 [2048, 14336], P(('groups', 'dp'), 'opt'), parts along dimension 0, may hold values from 1.024 to 10.24
Outputs:
- gate_grad: bfloat16 [2048, 14336], P(('groups', 'dp'), 'opt'), parts along dimension 0
- up_grad: bfloat16 [2048, 14336], P(('groups', 'dp'), 'opt'), parts along dimension 0
- weight_update: bfloat16 [8192, 14336], P(('groups', 'dp'), 'opt'), parts along dimension 0
There are 2 independent parts, one for each index of `groups`. A program takes and returns all parts, laid end to end along the dimension named above; an argument that names none is the same for every part. Nothing has to cross between parts.
All inputs are finite; a program needn't handle non-finite values.
Results may differ from a plain program's by a relative error of at most 0.006.
Values may be sent and summed in bfloat16 or wider, within the bound.
A program may use at most 192 MiB of HBM per device.

v0:
```python
import jax
import jax.numpy as jnp
from jax import lax
from jax.sharding import PartitionSpec as P

decay_first = 0.9
decay_second = 0.999
fix_first = 1.0 - 0.9**4
fix_second = 1.0 - 0.999**4
epsilon = 1e-08


def spread(block, axis, source):
    block = jnp.where(lax.axis_index(axis) == source, block, jnp.zeros_like(block))
    return lax.psum(block, axis)


def per_device(gate_pre, up_pre, cotangent, down_weight, projector, moment_first, moment_second):
    gate_wide = gate_pre.astype(jnp.float32)
    up_wide = up_pre.astype(jnp.float32)
    sigmoid_gate = jax.nn.sigmoid(gate_wide)
    swish_gate = gate_wide * sigmoid_gate
    hidden = (swish_gate * up_wide).astype(jnp.bfloat16)
    partial_proj = jnp.dot(cotangent, projector, preferred_element_type=jnp.float32)
    projected = lax.psum(partial_proj, "opt").astype(jnp.bfloat16)
    columns = projected
    lowrank_own = lax.psum_scatter(
        lax.dot_general(
            columns, hidden, (((0,), (0,)), ((), ())), preferred_element_type=jnp.float32
        ),
        "dp",
        scatter_dimension=0,
        tiled=True,
    )
    first = decay_first * moment_first + (1.0 - decay_first) * lowrank_own
    second = decay_second * moment_second + (1.0 - decay_second) * lowrank_own * lowrank_own
    direction = (first / fix_first / (jnp.sqrt(second / fix_second) + epsilon)).astype(jnp.bfloat16)
    full_cotangent = lax.all_gather(cotangent, "opt", axis=1, tiled=True)
    columns = full_cotangent
    hidden_grad = jnp.dot(
        columns,
        lax.all_gather(down_weight, "dp", axis=0, tiled=True),
        preferred_element_type=jnp.float32,
    )
    gate_grad = (
        hidden_grad * up_wide * sigmoid_gate * (1.0 + gate_wide * (1.0 - sigmoid_gate))
    ).astype(jnp.bfloat16)
    up_grad = (hidden_grad * swish_gate).astype(jnp.bfloat16)
    matching_rows = spread(projector, "opt", lax.axis_index("dp"))
    columns = matching_rows
    update_sum = jnp.dot(
        columns,
        lax.all_gather(direction, "dp", axis=0, tiled=True),
        preferred_element_type=jnp.float32,
    )
    return (gate_grad, up_grad, update_sum.astype(jnp.bfloat16))


def solution(mesh):
    in_specs = (
        P(("groups", "dp"), "opt"),
        P(("groups", "dp"), "opt"),
        P(("groups", "dp"), "opt"),
        P("dp", "opt"),
        P(("groups", "opt"), None),
        P(("groups", "dp"), "opt"),
        P(("groups", "dp"), "opt"),
    )
    out_specs = (P(("groups", "dp"), "opt"), P(("groups", "dp"), "opt"), P(("groups", "dp"), "opt"))
    return jax.shard_map(
        per_device, mesh=mesh, in_specs=in_specs, out_specs=out_specs, check_vma=False
    )
```

profile of v0, /device:TPU:3, one launch (start us, length us, event | category | flops | bytes accessed | tf_op | source)
XLA Modules:
  0.0 974.3 jit_solution(10304478737608354187)
XLA Ops:
  8.0 0.0 copy-start.1
  8.0 0.0 reduce-scatter.2.cloned.1.call-start
  8.1 2.6 fusion.18
  10.6 26.2 %all-reduce.4 = bf16[256,1024]{1,0:T(8,128)(2,1)S(1)} all-reduce(f32[256,1024]{1,0:T(8,128)S(1)} %fusion.18), channel_id=1, replica_groups=mesh['groups'=2,'dp'=4,'opt'=4] {'opt'}, use_global_device_ids=true, to_apply=%region_1.0 | all-reduce | flops 262144 | bytes 1572864 | tf_op jit(solution)/shard_map/psum | solution.py:25
  36.8 0.0 copy-done.1
  36.8 8.9 fusion.14
  45.8 0.0 copy-start
  45.8 0.0 reduce-scatter.2.cloned.1.call-update
  45.8 0.0 all-reduce.3.cloned.1.call-start
  45.8 1.5 copy-done
  47.4 1.5 broadcast_select_fusion
  48.8 0.0 all-reduce.3.cloned.1.call-update
  48.8 0.0 all-gather.8.cloned.1.call-start
  48.9 243.6 %reduce-scatter.2.cloned.1.call-done = f32[256,3584]{1,0:T(8,128)} async-done(((f32[1024,3584]{1,0:T(8,128)}), f32[256,3584]{1,0:T(8,128)}) %reduce-scatter.2.cloned.1.call-update) | async-done | bytes 3670032 | tf_op jit(solution)/shard_map/reduce_scatter | solution.py:27
  292.5 7.8 fusion.13
  300.3 0.0 all-gather.8.cloned.1.call-update
  300.3 0.0 all-gather.4.cloned.1.call-start
  300.3 0.7 all-gather.4.cloned.1.call-update
  301.0 0.2 all-gather.6.cloned.1.call-start
  301.3 0.3 all-gather.6.cloned.1.call-update
  301.6 0.0 copy-start.2
  301.6 0.0 all-reduce.3.cloned.1.call-done
  301.6 132.5 %all-gather.8.cloned.1.call-done = bf16[1024,3584]{1,0:T(8,128)(2,1)} async-done(((bf16[256,3584]{1,0:T(8,128)(2,1)}), bf16[1024,3584]{1,0:T(8,128)(2,1)}) %all-gather.8.cloned.1.call-update) | async-done | bytes 7340048 | tf_op jit(solution)/shard_map/all_gather | solution.py:53
  434.2 12.5 %convolution_convert_fusion = bf16[1024,3584]{1,0:T(8,128)(2,1)} fusion(bf16[1024,1024]{1,0:T(8,128)(2,1)} %all-reduce.3.cloned.1.call-done, bf16[1024,3584]{1,0:T(8,128)(2,1)} %all-gather.8.cloned.1.call-done), kind=kOutput, calls=%fused_computation | convolution fusion | flops 7519862784 | bytes 16777216 | tf_op jit(solution)/shard_map/dot_general | solution.py:51
  446.6 9.0 all-gather.4.cloned.1.call-done
  455.6 495.6 %all-gather.6.cloned.1.call-done = bf16[4096,3584]{1,0:T(8,128)(2,1)} async-done(((bf16[1024,3584]{1,0:T(8,128)(2,1)}), bf16[4096,3584]{1,0:T(8,128)(2,1)}) %all-gather.6.cloned.1.call-update) | async-done | bytes 29360144 | tf_op jit(solution)/shard_map/all_gather | solution.py:42
  951.2 0.0 copy-done.2
  951.2 15.9 %multiply_convert_fusion = (bf16[256,3584]{1,0:T(8,128)(2,1)}, bf16[256,3584]{1,0:T(8,128)(2,1)}) fusion(bf16[256,3584]{1,0:T(8,128)(2,1)S(1)} %copy-done.2, bf16[256,3584]{1,0:T(8,128)(2,1)} %param.8, bf16[256,4096]{1,0:T(8,128)(2,1)} %all-gather.4.cloned.1.call-done, bf16[4096,3584]{1,0:T(8,128)(2,1)} %all-gather.6.cloned.1.call-done), kind=kOutput, calls=%fused_computation.20 | convolution fusion | flops 7529955328 | bytes 38797312 | tf_op jit(solution)/shard_map/dot_general | solution.py:40
Async XLA Ops:
  8.0 28.8 %copy-start.1 = (bf16[256,3584]{1,0:T(8,128)(2,1)S(1)}, bf16[256,3584]{1,0:T(8,128)(2,1)}, u32[]{:S(2)}) copy-start(bf16[256,3584]{1,0:T(8,128)(2,1)} %param.7) | copy-start | bytes 5505028
  8.0 284.4 %reduce-scatter.2.cloned.1.call-start = ((), (), s32[]{:S(2)}) async-start(), calls=%async_computation.4 | async-start | bytes 18350080 | tf_op jit(solution)/shard_map/reduce_scatter | solution.py:27
  45.8 1.6 copy-start
  45.8 255.8 %all-reduce.3.cloned.1.call-start = ((), (), s32[]{:S(2)}) async-start(), calls=%async_computation.3 | async-start | bytes 4194304 | tf_op jit(solution)/shard_map/psum | solution.py:15
  48.8 385.3 %all-gather.8.cloned.1.call-start = ((), (), s32[]{:S(2)}) async-start(), calls=%async_computation.5 | async-start | bytes 9175040 | tf_op jit(solution)/shard_map/all_gather | solution.py:53
  300.3 155.3 %all-gather.4.cloned.1.call-start = ((), (), s32[]{:S(2)}) async-start(), calls=%async_computation.1 | async-start | bytes 2621440 | tf_op jit(solution)/shard_map/all_gather | solution.py:38
  301.0 650.2 %all-gather.6.cloned.1.call-start = ((), (), s32[]{:S(2)}) async-start(), calls=%async_computation.2 | async-start | bytes 36700160 | tf_op jit(solution)/shard_map/all_gather | solution.py:42
  301.6 649.6 %copy-start.2 = (bf16[256,3584]{1,0:T(8,128)(2,1)S(1)}, bf16[256,3584]{1,0:T(8,128)(2,1)}, u32[]{:S(2)}) copy-start(bf16[256,3584]{1,0:T(8,128)(2,1)} %param.7) | copy-start | bytes 5505028
Sparse Core Ops, SparseCore 0:
  45.9 246.4 reduce-scatter.1
  300.4 133.7 all-gather.7
  435.7 19.8 all-gather.3
  457.1 494.0 all-gather.5
Sparse Core Ops, SparseCore 1:
  49.2 51.0 all-reduce.2
where the time goes:
time: 976 us; the launch traced here: 974 us
  waiting for transfers between devices  882 us (90%)
  matrix products  39.9 us (4%)
  blocking collectives  26.2 us (3%)
  between operations  15.3 us (2%)
    all_gather x1, waiting for transfers between devices, per_device(): lax.all_gather(down_weight, 'dp', axis=0, tiled=True)  496 us
    reduce_scatter x1, waiting for transfers between devices, per_device(): lax.psum_scatter(lax.dot_general(columns, hidden, (((0,), (0,)), ((), ())...  244 us
    all_gather x1, waiting for transfers between devices, per_device(): lax.all_gather(direction, 'dp', axis=0, tiled=True)  133 us
    psum x1, blocking collectives, per_device(): projected = lax.psum(partial_proj, 'opt').astype(jnp.bfloat16)  26.2 us
  transfers between devices with their start and end apart: 5, of which 4 were waited for; matrix products, arithmetic and copies ran while one was open for 2% of the time, Pallas kernels for 0%

commit v1 on v0

v1 whole, which is shorter than its diff:
```python
import functools

import jax
import jax.numpy as jnp
from jax import lax
from jax.experimental import pallas as pl
from jax.experimental.pallas import tpu as pltpu
from jax.sharding import PartitionSpec as P

decay_first = 0.9
decay_second = 0.999
fix_first = 1.0 - 0.9**4
fix_second = 1.0 - 0.999**4
epsilon = 1e-08

MESH = pl.DeviceIdType.MESH
f32 = jnp.float32
bf16 = jnp.bfloat16


def kernel(n, m, C, CA, gate, up, cot, w, proj, m1, m2, gg_out, ug_out, wu_out,
           gate_v, up_v, cot_v, w_v, proj_v, m1_v, m2_v,
           hid, hidb, dirn, cot_all, pmatch, part, precv, pown, pall, hgb, lrb, stage,
           load, out_sem, wu_sem, c1s, c1r, c2s, c2r, pas, par, pbs, pbr, pzs, pzr, pms, pmr,
           hsr, hsl, hr, lrs, lrr, hgs, hgr, dsr, dsl, dr):
    CB = C - CA
    tok, ff = gate.shape
    cw = ff // C
    feat = w.shape[0]
    rn = m1.shape[0]
    rm = part.shape[0] // m
    tq = tok // m
    d = lax.axis_index("dp")
    o = lax.axis_index("opt")
    last = n - 1

    def cols(c):
        return pl.ds(pl.multiple_of(c * cw, cw), cw)

    def peer(z, q):
        return {"dp": z, "opt": q}

    def remote(src, dst, ss, rs, dev):
        return pltpu.make_async_remote_copy(
            src_ref=src, dst_ref=dst, send_sem=ss, recv_sem=rs, device_id=dev, device_id_type=MESH
        )

    def each(count, body):
        def step(i, carry):
            body(i)
            return carry

        lax.fori_loop(0, count, step, 0)

    loads = [
        pltpu.make_async_copy(src, dst, load.at[i])
        for i, (src, dst) in enumerate(
            ((gate, gate_v), (up, up_v), (cot, cot_v), (proj, proj_v), (w, w_v), (m1, m1_v), (m2, m2_v))
        )
    ]
    for copy in loads:
        copy.start()

    barrier = pltpu.get_barrier_semaphore()

    def greet(i):
        @pl.when(i != d * m + o)
        def _():
            pl.semaphore_signal(barrier, inc=1, device_id=peer(i // m, i % m), device_id_type=MESH)

    each(n * m, greet)

    def make_hidden(c, store, place):
        g = gate_v[:, cols(c)].astype(f32)
        u = up_v[:, cols(c)].astype(f32)
        value = (g * jax.nn.sigmoid(g) * u).astype(bf16)
        if store is hid:
            hid[d, :, cols(place)] = value
        else:
            hidb[:, cols(place)] = value

    loads[0].wait()
    loads[1].wait()
    make_hidden(0, hid, 0)
    pl.semaphore_wait(barrier, n * m - 1)

    def ag_right(buf, ss, rs, j, c):
        return remote(buf(j, c), buf(j, c), ss.at[c * n + j], rs.at[c * n + j], peer(d + 1, o))

    def ag_left(buf, ss, rs, j, c):
        return remote(buf(j, c), buf(j, c), ss.at[c * n + j], rs.at[c * n + j], peer(d - 1, o))

    def hid_at(j, c):
        return hid.at[j, :, cols(c)]

    def dir_at(j, c):
        return dirn.at[pl.ds(pl.multiple_of(j * rn, rn), rn), cols(c)]

    def ag_own(buf, sr, sl, rs, c):
        @pl.when(d < last)
        def _():
            ag_right(buf, sr, rs, d, c).start()

        @pl.when(d > 0)
        def _():
            ag_left(buf, sl, rs, d, c).start()

    def ag_relay(buf, sr, sl, rs, s, count):
        def hop(i):
            h = i + 1
            c = s - h
            ok = jnp.logical_and(c >= 0, c < count)

            @pl.when(jnp.logical_and(ok, d - h >= 0))
            def _():
                ag_left(buf, sl, rs, d - h, c).wait_recv()

                @pl.when(d < last)
                def _():
                    ag_right(buf, sr, rs, d - h, c).start()

            @pl.when(jnp.logical_and(ok, d + h <= last))
            def _():
                ag_right(buf, sr, rs, d + h, c).wait_recv()

                @pl.when(d > 0)
                def _():
                    ag_left(buf, sl, rs, d + h, c).start()

        each(n - 1, hop)

    def ag_drain(buf, sr, sl, rs, count):
        def chunk(c):
            def source(j):
                @pl.when(jnp.logical_and(d < last, j <= d))
                def _():
                    ag_right(buf, sr, rs, j, c).wait_send()

                @pl.when(jnp.logical_and(d > 0, j >= d))
                def _():
                    ag_left(buf, sl, rs, j, c).wait_send()

            each(n, source)

        each(count, chunk)

    def rs_right(buf, ss, rs, t, c):
        return remote(buf.at[t, :, cols(c)], buf.at[t, :, cols(c)], ss.at[c * n + t],
                      rs.at[c * (n + 1) + t], peer(d + 1, o))

    def rs_left(buf, ss, rs, t, c):
        slot = jnp.where(t == d - 1, n, t)
        return remote(buf.at[t, :, cols(c)], buf.at[slot, :, cols(c)], ss.at[c * n + t],
                      rs.at[c * (n + 1) + slot], peer(d - 1, o))

    def rs_arrived_left(buf, ss, rs, slot, c):
        remote(buf.at[slot, :, cols(c)], buf.at[slot, :, cols(c)], ss.at[c * n],
               rs.at[c * (n + 1) + slot], peer(d - 1, o)).wait_recv()

    def rs_arrived_right(buf, ss, rs, slot, c):
        remote(buf.at[slot, :, cols(c)], buf.at[slot, :, cols(c)], ss.at[c * n],
               rs.at[c * (n + 1) + slot], peer(d + 1, o)).wait_recv()

    def rs_step(buf, ss, rs, s, count, term):
        cr = s - d
        cl = s - (last - d)

        def hop(k):
            t = last - k

            @pl.when(jnp.logical_and(jnp.logical_and(cr >= 0, cr < count), t > d))
            def _():
                value = term(t, cr)

                @pl.when(d > 0)
                def _():
                    rs_arrived_left(buf, ss, rs, t, cr)
                    buf[t, :, cols(cr)] = (buf[t, :, cols(cr)].astype(f32) + value).astype(bf16)

                @pl.when(d == 0)
                def _():
                    buf[t, :, cols(cr)] = value.astype(bf16)

                rs_right(buf, ss, rs, t, cr).start()

            @pl.when(jnp.logical_and(jnp.logical_and(cl >= 0, cl < count), k < d))
            def _():
                value = term(k, cl)

                @pl.when(d < last)
                def _():
                    rs_arrived_right(buf, ss, rs, k, cl)
                    buf[k, :, cols(cl)] = (buf[k, :, cols(cl)].astype(f32) + value).astype(bf16)

                @pl.when(d == last)
                def _():
                    buf[k, :, cols(cl)] = value.astype(bf16)

                rs_left(buf, ss, rs, k, cl).start()

        each(n - 1, hop)

    def rs_take(buf, ss, rs, c, value):
        @pl.when(d > 0)
        def _():
            rs_arrived_left(buf, ss, rs, d, c)

        @pl.when(d == 0)
        def _():
            buf[d, :, cols(c)] = jnp.zeros(value.shape, bf16)

        @pl.when(d < last)
        def _():
            rs_arrived_right(buf, ss, rs, n, c)

        @pl.when(d == last)
        def _():
            buf[n, :, cols(c)] = jnp.zeros(value.shape, bf16)

        return value + buf[d, :, cols(c)].astype(f32) + buf[n, :, cols(c)].astype(f32)

    def rs_drain(buf, ss, rs, count):
        def chunk(c):
            def dest(t):
                @pl.when(t > d)
                def _():
                    rs_right(buf, ss, rs, t, c).wait_send()

                @pl.when(t < d)
                def _():
                    rs_left(buf, ss, rs, t, c).wait_send()

            each(n, dest)

        each(count, chunk)

    ag_own(hid_at, hsr, hsl, hr, 0)

    loads[2].wait()
    loads[3].wait()

    for q in range(m):
        part[q * rm:(q + 1) * rm, :] = lax.dot_general(
            proj_v[:, q * rm:(q + 1) * rm], cot_v[...], (((0,), (1,)), ((), ())),
            preferred_element_type=f32,
        )

    def part_rows(q):
        return part.at[pl.ds(pl.multiple_of(q * rm, rm), rm), :]

    def pa_send(q):
        return remote(part_rows(q), precv.at[o], pas.at[q], par.at[o], peer(d, q))

    def pa_recv(q):
        return remote(part_rows(q), precv.at[q], pas.at[q], par.at[q], peer(d, q))

    def c1_send(q):
        return remote(cot_v.at[pl.ds(pl.multiple_of(q * tq, tq), tq), :], cot_all.at[q, d],
                      c1s.at[q], c1r.at[d], peer(o, q))

    def others(body):
        def one(q):
            @pl.when(q != o)
            def _():
                body(q)

        each(m, one)

    others(lambda q: pa_send(q).start())

    def is_self(q):
        return jnp.logical_and(o == d, q == o)

    def c1_start(q):
        @pl.when(jnp.logical_not(is_self(q)))
        def _():
            c1_send(q).start()

    each(m, c1_start)

    @pl.when(o == d)
    def _():
        cot_all[o, d] = cot_v[pl.ds(pl.multiple_of(o * tq, tq), tq), :]

    def rest(c):
        make_hidden(c + 1, hid, c + 1)

    each(CA - 1, rest)

    def restb(c):
        make_hidden(c + CA, hidb, c)

    each(CB, restb)

    precv[o] = part[pl.ds(pl.multiple_of(o * rm, rm), rm), :]
    others(lambda q: pa_recv(q).wait_recv())
    total = precv[0]
    for q in range(1, m):
        total = total + precv[q]
    mine = total.astype(bf16)
    pown[o] = mine

    @pl.when(o == d)
    def _():
        pall[d] = mine

    def pb_send(q):
        return remote(pown.at[o], pown.at[o], pbs.at[q], pbr.at[o], peer(d, q))

    def pb_recv(q):
        return remote(pown.at[q], pown.at[q], pbs.at[q], pbr.at[q], peer(d, q))

    def pz_send(q):
        return remote(pown.at[o], pall.at[d], pzs.at[q], pzr.at[d], peer(o, q))

    others(lambda q: pb_send(q).start())

    def pz_start(q):
        @pl.when(jnp.logical_not(is_self(q)))
        def _():
            pz_send(q).start()

    each(m, pz_start)
    others(lambda q: pb_recv(q).wait_recv())

    def lr_term(t, c):
        return jnp.dot(pown[t], hidb[:, cols(c)], preferred_element_type=f32)

    def c2_send(q):
        return remote(cot_all.at[o], cot_all.at[o], c2s.at[q], c2r.at[o], peer(d, q))

    def c2_recv(q):
        return remote(cot_all.at[q], cot_all.at[q], c2s.at[q], c2r.at[q], peer(d, q))

    def from_layers(wait):
        def one(z):
            @pl.when(jnp.logical_or(z != d, o != d))
            def _():
                wait(z)

        each(n, one)

    def pm_send(q):
        return remote(proj_v, pmatch, pms.at[q], pmr, peer(d, q))

    def phase1(s):
        @pl.when(jnp.logical_and(s > 0, s < CA))
        def _():
            ag_own(hid_at, hsr, hsl, hr, s)

        rs_step(lrb, lrs, lrr, s, CB, lr_term)
        ag_relay(hid_at, hsr, hsl, hr, s, CA)

        @pl.when(s == 0)
        def _():
            from_layers(lambda z: remote(cot_all.at[o, z], cot_all.at[o, z], c1s.at[0], c1r.at[z],
                                         peer(d, lax.rem(o + 1, m))).wait_recv())
            others(lambda q: c2_send(q).start())

            @pl.when(o == d)
            def _():
                others(lambda q: pm_send(q).start())
                pmatch[...] = proj_v[...]

    each(max(CA + n - 1, CB + n - 1), phase1)

    from_layers(lambda z: remote(pall.at[z], pall.at[z], pzs.at[0], pzr.at[z],
                                 peer(d, lax.rem(o + 1, m))).wait_recv())
    others(lambda q: c2_recv(q).wait_recv())
    for i in (4, 5, 6):
        loads[i].wait()

    @pl.when(o != d)
    def _():
        remote(proj_v, pmatch, pms.at[0], pmr, peer(d, d)).wait_recv()

    def hg_term(t, c):
        rows = cot_all[:, pl.ds(t, 1)].reshape(tok, feat)
        return jnp.dot(rows, w_v[:, cols(c)], preferred_element_type=f32)

    def adam(lowrank, c):
        first = decay_first * m1_v[:, cols(c)] + (1.0 - decay_first) * lowrank
        second = decay_second * m2_v[:, cols(c)] + (1.0 - decay_second) * lowrank * lowrank
        value = (first / fix_first / (jnp.sqrt(second / fix_second) + epsilon)).astype(bf16)
        dirn[pl.ds(pl.multiple_of(d * rn, rn), rn), cols(c)] = value

    def out_copies(c):
        return (
            pltpu.make_async_copy(gate_v.at[:, cols(c)], gg_out.at[:, cols(c)], out_sem.at[2 * c]),
            pltpu.make_async_copy(up_v.at[:, cols(c)], ug_out.at[:, cols(c)], out_sem.at[2 * c + 1]),
        )

    def wu_copy(c):
        slot = lax.rem(c, 2)
        return pltpu.make_async_copy(stage.at[slot], wu_out.at[:, cols(c)], wu_sem.at[slot])

    rows_step = min(256, feat)

    def phase2(s):
        rs_step(hgb, hgs, hgr, s, C, hg_term)

        @pl.when(s < CA)
        def _():
            def add(j, acc):
                return acc + jnp.dot(pall[j], hid[j, :, cols(s)], preferred_element_type=f32)

            adam(lax.fori_loop(0, n, add, jnp.zeros((rn, cw), f32)), s)

        @pl.when(jnp.logical_and(s >= CA, s < C))
        def _():
            c = s - CA
            adam(rs_take(lrb, lrs, lrr, c, lr_term(d, c)), s)

        @pl.when(s < C)
        def _():
            ag_own(dir_at, dsr, dsl, dr, s)

        ag_relay(dir_at, dsr, dsl, dr, s, C)

        c = s - last

        @pl.when(c >= 0)
        def _():
            g = gate_v[:, cols(c)].astype(f32)
            u = up_v[:, cols(c)].astype(f32)
            sig = jax.nn.sigmoid(g)
            grad = rs_take(hgb, hgs, hgr, c, hg_term(d, c))
            gate_v[:, cols(c)] = (grad * u * sig * (1.0 + g * (1.0 - sig))).astype(bf16)
            up_v[:, cols(c)] = (grad * (g * sig)).astype(bf16)
            for copy in out_copies(c):
                copy.start()

            @pl.when(c >= 2)
            def _():
                wu_copy(c - 2).wait()

            slot = lax.rem(c, 2)

            def tile(i):
                rows = pl.ds(pl.multiple_of(i * rows_step, rows_step), rows_step)
                stage[slot, rows, :] = jnp.dot(
                    pmatch[rows, :], dirn[:, cols(c)], preferred_element_type=f32
                ).astype(bf16)

            each(feat // rows_step, tile)
            wu_copy(c).start()

    each(C + n - 1, phase2)

    ag_drain(hid_at, hsr, hsl, hr, CA)
    rs_drain(lrb, lrs, lrr, CB)
    rs_drain(hgb, hgs, hgr, C)
    ag_drain(dir_at, dsr, dsl, dr, C)
    others(lambda q: pa_send(q).wait_send())
    others(lambda q: pb_send(q).wait_send())
    others(lambda q: c2_send(q).wait_send())

    def tail(q):
        @pl.when(jnp.logical_not(is_self(q)))
        def _():
            c1_send(q).wait_send()
            pz_send(q).wait_send()

    each(m, tail)

    @pl.when(o == d)
    def _():
        others(lambda q: pm_send(q).wait_send())

    def finish(c):
        for copy in out_copies(c):
            copy.wait()

    each(C, finish)
    wu_copy(C - 2).wait()
    wu_copy(C - 1).wait()


def per_device(n, m, gate_pre, up_pre, cotangent, down_weight, projector, moment_first, moment_second):
    tok, ff = gate_pre.shape
    feat, rank = projector.shape
    rn = moment_first.shape[0]
    C, CA = 7, 4
    CB = C - CA
    cw = ff // C
    dma = pltpu.SemaphoreType.DMA
    vmem = pltpu.VMEM
    return pl.pallas_call(
        functools.partial(kernel, n, m, C, CA),
        out_shape=(
            jax.ShapeDtypeStruct((tok, ff), bf16),
            jax.ShapeDtypeStruct((tok, ff), bf16),
            jax.ShapeDtypeStruct((feat, ff), bf16),
        ),
        in_specs=[pl.BlockSpec(memory_space=pl.ANY)] * 7,
        out_specs=[pl.BlockSpec(memory_space=pl.ANY)] * 3,
        scratch_shapes=[
            vmem((tok, ff), bf16), vmem((tok, ff), bf16), vmem(cotangent.shape, bf16),
            vmem((feat, ff), bf16), vmem((feat, rank), bf16),
            vmem((rn, ff), f32), vmem((rn, ff), f32),
            vmem((n, tok, CA * cw), bf16), vmem((tok, CB * cw), bf16), vmem((rank, ff), bf16),
            vmem((m, n, tok // m, feat), bf16), vmem((feat, rank), bf16),
            vmem((rank, tok), f32), vmem((m, rank // m, tok), f32),
            vmem((m, rank // m, tok), bf16), vmem((n, rn, tok), bf16),
            vmem((n + 1, tok, ff), bf16), vmem((n + 1, rn, CB * cw), bf16),
            vmem((2, feat, cw), bf16),
            dma((7,)), dma((2 * C,)), dma((2,)),
            dma((m,)), dma((n,)), dma((m,)), dma((m,)), dma((m,)), dma((m,)), dma((m,)), dma((m,)),
            dma((m,)), dma((n,)), dma((m,)), dma,
            dma((CA * n,)), dma((CA * n,)), dma((CA * n,)),
            dma((CB * n,)), dma((CB * (n + 1),)), dma((C * n,)), dma((C * (n + 1),)),
            dma((C * n,)), dma((C * n,)), dma((C * n,)),
        ],
        compiler_params=pltpu.CompilerParams(
            collective_id=0, has_side_effects=True, vmem_limit_bytes=62 * 1024 * 1024
        ),
    )(gate_pre, up_pre, cotangent, down_weight, projector, moment_first, moment_second)


def solution(mesh):
    in_specs = (
        P(("groups", "dp"), "opt"),
        P(("groups", "dp"), "opt"),
        P(("groups", "dp"), "opt"),
        P("dp", "opt"),
        P(("groups", "opt"), None),
        P(("groups", "dp"), "opt"),
        P(("groups", "dp"), "opt"),
    )
    out_specs = (P(("groups", "dp"), "opt"), P(("groups", "dp"), "opt"), P(("groups", "dp"), "opt"))
    return jax.shard_map(
        functools.partial(per_device, mesh.shape["dp"], mesh.shape["opt"]),
        mesh=mesh, in_specs=in_specs, out_specs=out_specs, check_vma=False,
    )
```

time: 976 us -> 335 us (0.34)
  waiting for transfers between devices: 882 us -> 0 us
  Pallas kernels: 0 us -> 321 us
  matrix products: 39.9 us -> 0 us
  blocking collectives: 26.2 us -> 0 us
  between operations: 15.3 us -> 0.65 us
    all_gather x3 -> x0, waiting for transfers between devices: 637 us -> none  [the longest x1 496 us: per_device(): lax.all_gather(down_weight, 'dp', axis=0, tiled=True)]
    pallas_call x0 -> x1, Pallas kernels: none -> 321 us  [per_device(): pl.pallas_call(functools.partial(kernel, n, m, C, CA), out_shape=(jax.Sha...]
    reduce_scatter x1 -> x0, waiting for transfers between devices: 244 us -> none  [per_device(): lax.psum_scatter(lax.dot_general(columns, hidden, (((0,), (0,)), ((), ())...]
    dot_general x4 -> x0, matrix products: 39.9 us -> none  [the longest x1 15.9 us: per_device(): jnp.dot(columns, lax.all_gather(down_weight, 'dp', axis=0, tiled=True), p...]
    psum x1 -> x0, blocking collectives: 26.2 us -> none  [per_device(): projected = lax.psum(partial_proj, 'opt').astype(jnp.bfloat16)]
  transfers between devices with their start and end apart: 5 -> 0, of which waited for: 4 -> 0; matrix products, arithmetic and copies ran while one was open for 2% -> 0% of each run, Pallas kernels for 0% -> 0%
where the time goes in v1:
time: 335 us; the launch traced here: 333 us
  Pallas kernels  321 us (96%)
  local copies, waits for them, and re-layouts  10.8 us (3%)
    pallas_call x1, Pallas kernels, per_device(): pl.pallas_call(functools.partial(kernel, n, m, C, CA), out_shape=(jax.Sha...  321 us
    unnamed x5, local copies, waits for them, and re-layouts  10.8 us

profile of v1, /device:TPU:3, one launch (start us, length us, event | category | flops | bytes accessed | tf_op | source)
XLA Modules:
  0.0 332.8 jit_solution(5613342533931234526)
XLA Ops:
  0.6 321.3 %shard_map.94 = (bf16[256,3584]{1,0:T(8,128)(2,1)}, bf16[256,3584]{1,0:T(8,128)(2,1)}, bf16[1024,3584]{1,0:T(8,128)(2,1)}) custom-call(bf16[256,3584]{1,0:T(8,128)(2,1)} %gate.1, bf16[256,3584]{1,0:T(8,128)(2,1)} %up.1, bf16[256,1024]{1,0:T(8,128)(2,1)} %cot.1, bf16[1024,3584]{1,0:T(8,128)(2,1)} %w.1, bf16[1024,1024]{1,0:T(8,128)(2,1)} %proj.1, ...), custom_call_target="tpu_custom_call" | custom-call | tf_op jit(solution)/shard_map/pallas_call | solution.py:488
  322.0 0.0 copy-start
  322.0 3.0 copy.13
  325.0 0.0 copy-done
  325.0 1.2 copy.14
  326.2 6.6 %copy.15 = bf16[1024,3584]{1,0:T(8,128)(2,1)} copy(bf16[1024,3584]{1,0:T(8,128)(2,1)} %get-tuple-element.8) | data formatting | bytes 14680064
Async XLA Ops:
  322.0 3.0 copy-start

commit v2 on v1

--- a/solution.py
+++ b/solution.py
@@ -18,10 +18,10 @@
 bf16 = jnp.bfloat16
 
 
-def kernel(n, m, C, CA, gate, up, cot, w, proj, m1, m2, gg_out, ug_out, wu_out,
+def kernel(n, m, C, CA, lag, sp, gate, up, cot, w, proj, m1, m2, gg_out, ug_out, wu_out,
            gate_v, up_v, cot_v, w_v, proj_v, m1_v, m2_v,
            hid, hidb, dirn, cot_all, pmatch, part, precv, pown, pall, hgb, lrb, stage,
-           load, out_sem, wu_sem, c1s, c1r, c2s, c2r, pas, par, pbs, pbr, pzs, pzr, pms, pmr,
+           load, out_sem, wu_sem, c1s, c1r, c2s, c2r, pas, par, pbs, pbr, pzs, pzr, p3s, p3r, pms, pmr,
            hsr, hsl, hr, lrs, lrr, hgs, hgr, dsr, dsl, dr):
     CB = C - CA
     tok, ff = gate.shape
@@ -108,7 +108,7 @@
     def ag_relay(buf, sr, sl, rs, s, count):
         def hop(i):
             h = i + 1
-            c = s - h
+            c = s - lag * h
             ok = jnp.logical_and(c >= 0, c < count)
 
             @pl.when(jnp.logical_and(ok, d - h >= 0))
@@ -162,8 +162,8 @@
                rs.at[c * (n + 1) + slot], peer(d + 1, o)).wait_recv()
 
     def rs_step(buf, ss, rs, s, count, term):
-        cr = s - d
-        cl = s - (last - d)
+        cr = s - lag * d
+        cl = s - lag * (last - d)
 
         def hop(k):
             t = last - k
@@ -300,9 +300,14 @@
     mine = total.astype(bf16)
     pown[o] = mine
 
-    @pl.when(o == d)
+    pq = rm // sp
+
+    def piece(q):
+        return pl.ds(pl.multiple_of(q * pq, pq), pq)
+
+    @pl.when(jnp.logical_and(o == d, o < sp))
     def _():
-        pall[d] = mine
+        pall[d, piece(o), :] = pown[o, piece(o), :]
 
     def pb_send(q):
         return remote(pown.at[o], pown.at[o], pbs.at[q], pbr.at[o], peer(d, q))
@@ -311,7 +316,13 @@
         return remote(pown.at[q], pown.at[q], pbs.at[q], pbr.at[q], peer(d, q))
 
     def pz_send(q):
-        return remote(pown.at[o], pall.at[d], pzs.at[q], pzr.at[d], peer(o, q))
+        return remote(pown.at[o, piece(q), :], pall.at[d, piece(q), :], pzs.at[q], pzr.at[d], peer(o, q))
+
+    def p3_send(q):
+        return remote(pall.at[:, piece(o), :], pall.at[:, piece(o), :], p3s.at[q], p3r.at[o], peer(d, q))
+
+    def p3_recv(q):
+        return remote(pall.at[:, piece(q), :], pall.at[:, piece(q), :], p3s.at[q], p3r.at[q], peer(d, q))
 
     others(lambda q: pb_send(q).start())
 
@@ -320,7 +331,7 @@
         def _():
             pz_send(q).start()
 
-    each(m, pz_start)
+    each(sp, pz_start)
     others(lambda q: pb_recv(q).wait_recv())
 
     def lr_term(t, c):
@@ -351,21 +362,31 @@
         rs_step(lrb, lrs, lrr, s, CB, lr_term)
         ag_relay(hid_at, hsr, hsl, hr, s, CA)
 
-        @pl.when(s == 0)
+        @pl.when(s == 2)
         def _():
             from_layers(lambda z: remote(cot_all.at[o, z], cot_all.at[o, z], c1s.at[0], c1r.at[z],
                                          peer(d, lax.rem(o + 1, m))).wait_recv())
             others(lambda q: c2_send(q).start())
 
+            @pl.when(o < sp)
+            def _():
+                from_layers(lambda z: remote(pall.at[z, piece(o), :], pall.at[z, piece(o), :], pzs.at[0],
+                                             pzr.at[z], peer(d, lax.rem(o + 1, m))).wait_recv())
+                others(lambda q: p3_send(q).start())
+
             @pl.when(o == d)
             def _():
                 others(lambda q: pm_send(q).start())
                 pmatch[...] = proj_v[...]
 
-    each(max(CA + n - 1, CB + n - 1), phase1)
-
-    from_layers(lambda z: remote(pall.at[z], pall.at[z], pzs.at[0], pzr.at[z],
-                                 peer(d, lax.rem(o + 1, m))).wait_recv())
+    each(max(CA, CB) + lag * last, phase1)
+
+    def p3_wait(q):
+        @pl.when(q < sp)
+        def _():
+            p3_recv(q).wait_recv()
+
+    others(p3_wait)
     others(lambda q: c2_recv(q).wait_recv())
     for i in (4, 5, 6):
         loads[i].wait()
@@ -417,7 +438,7 @@
 
         ag_relay(dir_at, dsr, dsl, dr, s, C)
 
-        c = s - last
+        c = s - lag * last
 
         @pl.when(c >= 0)
         def _():
@@ -445,7 +466,7 @@
             each(feat // rows_step, tile)
             wu_copy(c).start()
 
-    each(C + n - 1, phase2)
+    each(C + lag * last, phase2)
 
     ag_drain(hid_at, hsr, hsl, hr, CA)
     rs_drain(lrb, lrs, lrr, CB)
@@ -459,9 +480,16 @@
         @pl.when(jnp.logical_not(is_self(q)))
         def _():
             c1_send(q).wait_send()
-            pz_send(q).wait_send()
+
+            @pl.when(q < sp)
+            def _():
+                pz_send(q).wait_send()
 
     each(m, tail)
+
+    @pl.when(o < sp)
+    def _():
+        others(lambda q: p3_send(q).wait_send())
 
     @pl.when(o == d)
     def _():
@@ -480,13 +508,14 @@
     tok, ff = gate_pre.shape
     feat, rank = projector.shape
     rn = moment_first.shape[0]
-    C, CA = 7, 4
+    C, CA, lag = (14, 7, 1) if ff % (14 * 128) == 0 else (7, 4, 1)
+    sp = min(m, rank // m // 16)
     CB = C - CA
     cw = ff // C
     dma = pltpu.SemaphoreType.DMA
     vmem = pltpu.VMEM
     return pl.pallas_call(
-        functools.partial(kernel, n, m, C, CA),
+        functools.partial(kernel, n, m, C, CA, lag, sp),
         out_shape=(
             jax.ShapeDtypeStruct((tok, ff), bf16),
             jax.ShapeDtypeStruct((tok, ff), bf16),
@@ -506,7 +535,7 @@
             vmem((2, feat, cw), bf16),
             dma((7,)), dma((2 * C,)), dma((2,)),
             dma((m,)), dma((n,)), dma((m,)), dma((m,)), dma((m,)), dma((m,)), dma((m,)), dma((m,)),
-            dma((m,)), dma((n,)), dma((m,)), dma,
+            dma((m,)), dma((n,)), dma((m,)), dma((m,)), dma((m,)), dma,
             dma((CA * n,)), dma((CA * n,)), dma((CA * n,)),
             dma((CB * n,)), dma((CB * (n + 1),)), dma((C * n,)), dma((C * (n + 1),)),
             dma((C * n,)), dma((C * n,)), dma((C * n,)),

time: 335 us -> 318 us (0.949)
  Pallas kernels: 321 us -> 303 us
    pallas_call x1, Pallas kernels: 321 us -> 303 us  [per_device(): pl.pallas_call(functools.partial(kernel, n, m, C, CA, lag, sp), out_shape...]
where the time goes in v2:
time: 318 us; the launch traced here: 315 us
  Pallas kernels  303 us (95%)
  local copies, waits for them, and re-layouts  10.8 us (3%)
    pallas_call x1, Pallas kernels, per_device(): pl.pallas_call(functools.partial(kernel, n, m, C, CA, lag, sp), out_shape...  303 us
    unnamed x5, local copies, waits for them, and re-layouts  10.8 us

profile of v2, /device:TPU:3, one launch (start us, length us, event | category | flops | bytes accessed | tf_op | source)
XLA Modules:
  0.0 314.7 jit_solution(12865340308525040146)
XLA Ops:
  0.6 303.2 %shard_map.94 = (bf16[256,3584]{1,0:T(8,128)(2,1)}, bf16[256,3584]{1,0:T(8,128)(2,1)}, bf16[1024,3584]{1,0:T(8,128)(2,1)}) custom-call(bf16[256,3584]{1,0:T(8,128)(2,1)} %gate.1, bf16[256,3584]{1,0:T(8,128)(2,1)} %up.1, bf16[256,1024]{1,0:T(8,128)(2,1)} %cot.1, bf16[1024,3584]{1,0:T(8,128)(2,1)} %w.1, bf16[1024,1024]{1,0:T(8,128)(2,1)} %proj.1, ...), custom_call_target="tpu_custom_call" | custom-call | tf_op jit(solution)/shard_map/pallas_call | solution.py:517
  303.8 0.0 copy-start
  303.8 3.0 copy.13
  306.8 0.0 copy-done
  306.8 1.2 copy.14
  308.1 6.6 %copy.15 = bf16[1024,3584]{1,0:T(8,128)(2,1)} copy(bf16[1024,3584]{1,0:T(8,128)(2,1)} %get-tuple-element.8) | data formatting | bytes 14680064
Async XLA Ops:
  303.8 3.0 copy-start

commit v3 on v2

--- a/solution.py
+++ b/solution.py
@@ -379,7 +379,9 @@
                 others(lambda q: pm_send(q).start())
                 pmatch[...] = proj_v[...]
 
-    each(max(CA, CB) + lag * last, phase1)
+    ahead = max(CA, lag * last)
+    steps1 = max(CA, CB) + lag * last
+    each(ahead, phase1)
 
     def p3_wait(q):
         @pl.when(q < sp)
@@ -418,8 +420,6 @@
     rows_step = min(256, feat)
 
     def phase2(s):
-        rs_step(hgb, hgs, hgr, s, C, hg_term)
-
         @pl.when(s < CA)
         def _():
             def add(j, acc):
@@ -436,6 +436,7 @@
         def _():
             ag_own(dir_at, dsr, dsl, dr, s)
 
+        rs_step(hgb, hgs, hgr, s, C, hg_term)
         ag_relay(dir_at, dsr, dsl, dr, s, C)
 
         c = s - lag * last
@@ -466,7 +467,14 @@
             each(feat // rows_step, tile)
             wu_copy(c).start()
 
-    each(C + lag * last, phase2)
+    def both(i):
+        @pl.when(i + ahead < steps1)
+        def _():
+            phase1(i + ahead)
+
+        phase2(i)
+
+    each(max(C + lag * last, steps1 - ahead), both)
 
     ag_drain(hid_at, hsr, hsl, hr, CA)
     rs_drain(lrb, lrs, lrr, CB)

time: 318 us -> 306 us (0.962)
  Pallas kernels: 303 us -> 294 us
    pallas_call x1, Pallas kernels: 303 us -> 294 us  [per_device(): pl.pallas_call(functools.partial(kernel, n, m, C, CA, lag, sp), out_shape...]
where the time goes in v3:
time: 306 us
  Pallas kernels  294 us (96%)
  local copies, waits for them, and re-layouts  10.8 us (4%)
    pallas_call x1, Pallas kernels, per_device(): pl.pallas_call(functools.partial(kernel, n, m, C, CA, lag, sp), out_shape...  294 us
    unnamed x5, local copies, waits for them, and re-layouts  10.8 us

profile of v3, /device:TPU:3, one launch (start us, length us, event | category | flops | bytes accessed | tf_op | source)
XLA Modules:
  0.0 305.8 jit_solution(3603197340260250922)
XLA Ops:
  0.6 294.3 %shard_map.94 = (bf16[256,3584]{1,0:T(8,128)(2,1)}, bf16[256,3584]{1,0:T(8,128)(2,1)}, bf16[1024,3584]{1,0:T(8,128)(2,1)}) custom-call(bf16[256,3584]{1,0:T(8,128)(2,1)} %gate.1, bf16[256,3584]{1,0:T(8,128)(2,1)} %up.1, bf16[256,1024]{1,0:T(8,128)(2,1)} %cot.1, bf16[1024,3584]{1,0:T(8,128)(2,1)} %w.1, bf16[1024,1024]{1,0:T(8,128)(2,1)} %proj.1, ...), custom_call_target="tpu_custom_call" | custom-call | tf_op jit(solution)/shard_map/pallas_call | solution.py:525
  294.9 0.0 copy-start
  294.9 3.0 copy.13
  297.9 0.0 copy-done
  297.9 1.2 copy.14
  299.2 6.6 %copy.15 = bf16[1024,3584]{1,0:T(8,128)(2,1)} copy(bf16[1024,3584]{1,0:T(8,128)(2,1)} %get-tuple-element.8) | data formatting | bytes 14680064
Async XLA Ops:
  294.9 3.0 copy-start

commit v4 on v3

--- a/solution.py
+++ b/solution.py
@@ -436,8 +436,8 @@
         def _():
             ag_own(dir_at, dsr, dsl, dr, s)
 
+        ag_relay(dir_at, dsr, dsl, dr, s, C)
         rs_step(hgb, hgs, hgr, s, C, hg_term)
-        ag_relay(dir_at, dsr, dsl, dr, s, C)
 
         c = s - lag * last
 

time: 306 us -> 304 us (level)
  no operation moved by 1% of the time
where the time goes in v4:
time: 304 us
  Pallas kernels  292 us (96%)
  local copies, waits for them, and re-layouts  10.8 us (4%)
    pallas_call x1, Pallas kernels, per_device(): pl.pallas_call(functools.partial(kernel, n, m, C, CA, lag, sp), out_shape...  292 us
    unnamed x5, local copies, waits for them, and re-layouts  10.8 us

profile of v4, /device:TPU:3, one launch (start us, length us, event | category | flops | bytes accessed | tf_op | source)
XLA Modules:
  0.0 303.7 jit_solution(10395488167378394915)
XLA Ops:
  0.6 292.3 %shard_map.94 = (bf16[256,3584]{1,0:T(8,128)(2,1)}, bf16[256,3584]{1,0:T(8,128)(2,1)}, bf16[1024,3584]{1,0:T(8,128)(2,1)}) custom-call(bf16[256,3584]{1,0:T(8,128)(2,1)} %gate.1, bf16[256,3584]{1,0:T(8,128)(2,1)} %up.1, bf16[256,1024]{1,0:T(8,128)(2,1)} %cot.1, bf16[1024,3584]{1,0:T(8,128)(2,1)} %w.1, bf16[1024,1024]{1,0:T(8,128)(2,1)} %proj.1, ...), custom_call_target="tpu_custom_call" | custom-call | tf_op jit(solution)/shard_map/pallas_call | solution.py:525
  292.9 0.0 copy-start
  292.9 3.0 copy.13
  295.9 0.0 copy-done
  295.9 1.2 copy.14
  297.1 6.6 %copy.15 = bf16[1024,3584]{1,0:T(8,128)(2,1)} copy(bf16[1024,3584]{1,0:T(8,128)(2,1)} %get-tuple-element.8) | data formatting | bytes 14680064
Async XLA Ops:
  292.9 3.0 copy-start
